TPU v7x, 128 devices: a whole 4x4x4 slice. The times are simulated.
128 devices in a mesh: dp: 32 (over x, y, core), tensor: 4 (over z).
Axes of the slice: x: 4, y: 4, z: 4, core: 2. Of those that a mesh axis runs over, the one named last changes fastest.
Arguments:
- gradient: bfloat16 [8192, 16384], P('dp', 'tensor')
- block_slot: int32 [8, 4, 4], replicated, may hold values from 0 to 3, as said below
- left_factor: float32 [128, 1024, 1024], P(('dp', 'tensor')), as said below
- right_factor: float32 [128, 1024, 1024], P(('dp', 'tensor')), as said below
- left_root: bfloat16 [128, 1024, 1024], P(('dp', 'tensor')), as said below
- right_root: bfloat16 [128, 1024, 1024], P(('dp', 'tensor')), as said below
Outputs:
- update: bfloat16 [8192, 16384], P('dp', 'tensor')
- new_left: float32 [128, 1024, 1024], P(('dp', 'tensor'))
- new_right: float32 [128, 1024, 1024], P(('dp', 'tensor'))
Inputs may be any that keep to these rules, and one draw needn't show every extreme that they name: For each row block and each tensor index e, block_slot[i, e, :] is a permutation of 0 to 3. `left_factor`: every block is symmetric. `right_factor`: every block is symmetric. `left_root`: every block is symmetric. `right_root`: every block is symmetric.
All inputs are finite; a program needn't handle non-finite values.
Results may differ from a plain program's by a relative error of at most 0.0049.
Values may be sent and summed in bfloat16 or wider, within the bound.
A program may use at most 128 MiB of HBM per device.

v0:
```python
import jax
import jax.numpy as jnp
from jax import lax
from jax.sharding import PartitionSpec as P

B = 1024


def shifted(value, axis, steps):
    count = lax.axis_size(axis)
    first, last = (max(0, -steps), min(count, count - steps))
    return lax.ppermute(value, axis, [(source, source + steps) for source in range(first, last)])


def route_direct(buffer, member, back):
    group_size = buffer.shape[0]
    received = [lax.dynamic_index_in_dim(buffer, member, 0, keepdims=False)]
    for offset in range(1, group_size):
        leaving = lax.dynamic_index_in_dim(
            buffer, (member + offset) % group_size, 0, keepdims=False
        )
        if back:
            nearer = shifted(leaving, "dp", offset)
            farther = shifted(leaving, "dp", offset - group_size)
        else:
            nearer = shifted(leaving, "dp", offset)
            farther = shifted(leaving, "dp", offset - group_size)
        received.append(jnp.where(member >= offset, nearer, farther))
    stacked = jnp.stack(received)
    return jnp.take(stacked, (member - jnp.arange(group_size)) % group_size, axis=0)


def route_pieces(buffer, member, back):
    return route_direct(buffer, member, back)


def per_device(gradient, block_slot, left_factor, right_factor, left_root, right_root):
    row_count = gradient.shape[0]
    tensors = lax.axis_size("tensor")
    group_size = B // row_count
    per_owner = left_factor.shape[0]
    member = lax.axis_index("dp") % group_size
    row_block = lax.axis_index("dp") // group_size
    column_owner = lax.axis_index("tensor")
    arrived = lax.all_to_all(gradient, "tensor", split_axis=1, concat_axis=0, tiled=True)
    by_source = arrived.reshape(tensors, row_count, B)
    slot_order = block_slot[row_block, column_owner]
    outgoing = jnp.take(by_source, slot_order, axis=0).reshape(group_size, per_owner, row_count, B)
    routed = route_pieces(outgoing, member, False)
    blocks = jnp.transpose(routed, (1, 0, 2, 3)).reshape(per_owner, B, B)
    new_left = left_factor + jnp.einsum(
        "qab,qcb->qac", blocks, blocks, preferred_element_type=jnp.float32
    )
    new_right = right_factor + jnp.einsum(
        "qba,qbc->qac", blocks, blocks, preferred_element_type=jnp.float32
    )
    half_product = jnp.einsum(
        "qab,qbc->qac", left_root, blocks, preferred_element_type=jnp.float32
    ).astype(jnp.bfloat16)
    preconditioned = jnp.einsum(
        "qab,qbc->qac", half_product, right_root, preferred_element_type=jnp.float32
    )
    wide_blocks = blocks.astype(jnp.float32)
    grad_square = jnp.mean(wide_blocks * wide_blocks, axis=(1, 2))
    graft_scale = jnp.sqrt(
        grad_square / (jnp.mean(preconditioned * preconditioned, axis=(1, 2)) + 1e-06)
    )
    results = (preconditioned * graft_scale[:, None, None]).astype(jnp.bfloat16)
    leaving_pieces = jnp.transpose(
        results.reshape(per_owner, group_size, row_count, B), (1, 0, 2, 3)
    )
    returned = route_pieces(leaving_pieces, member, True)
    by_position = returned.reshape(tensors, row_count, B)
    positions = jnp.arange(tensors)
    inverse = jnp.sum(
        jnp.where(slot_order[None, :] == positions[:, None], positions[None, :], 0), axis=1
    )
    by_slot = jnp.take(by_position, inverse, axis=0).reshape(tensors * row_count, B)
    update = lax.all_to_all(by_slot, "tensor", split_axis=0, concat_axis=1, tiled=True)
    return (update, new_left, new_right)


def solution(mesh):
    placed = (
        P("dp", "tensor"),
        P(),
        P(("dp", "tensor"), None, None),
        P(("dp", "tensor"), None, None),
        P(("dp", "tensor"), None, None),
        P(("dp", "tensor"), None, None),
    )
    return jax.shard_map(
        per_device,
        mesh=mesh,
        in_specs=placed,
        out_specs=(
            P("dp", "tensor"),
            P(("dp", "tensor"), None, None),
            P(("dp", "tensor"), None, None),
        ),
        check_vma=False,
    )
```

profile of v0, /device:TPU:3, one launch (start us, length us, event | category | flops | bytes accessed | tf_op | source)
XLA Modules:
  0.0 203.9 jit_solution(10472278894338643012)
XLA Ops:
  0.6 0.0 copy-start
  0.6 4.2 %copy.21 = bf16[256,4096]{0,1:T(8,128)(2,1)} copy(bf16[256,4096]{1,0:T(8,128)(2,1)} %param.10) | data formatting | bytes 4194304 | tf_op args[0]
  4.9 3.9 %copy.22 = bf16[256,4,1024]{2,0,1:T(8,128)(2,1)} copy(bf16[256,4,1024]{0,2,1:T(8,128)(2,1)} %bitcast.70) | data formatting | bytes 4194304 | tf_op jit(solution)/shard_map/all_to_all | solution.py:45
  8.8 5.0 %all-to-all-start = ((bf16[256,4,1024]{2,0,1:T(8,128)(2,1)}), bf16[256,4,1024]{2,0,1:T(8,128)(2,1)}, u32[]{:S(2)}, u32[]{:S(2)}) async-start(bf16[256,4,1024]{2,0,1:T(8,128)(2,1)} %copy.22), calls=%async_computation | async-start | bytes 4194304 | tf_op jit(solution)/shard_map/all_to_all | solution.py:45
  13.8 0.9 fusion.11
  14.7 24.8 %all-to-all-done = bf16[256,4,1024]{2,0,1:T(8,128)(2,1)} async-done(((bf16[256,4,1024]{2,0,1:T(8,128)(2,1)}), bf16[256,4,1024]{2,0,1:T(8,128)(2,1)}, u32[]{:S(2)}, u32[]{:S(2)}) %all-to-all-start) | async-done | bytes 2097184 | tf_op jit(solution)/shard_map/all_to_all | solution.py:45
  39.5 3.6 %gather_fusion = bf16[4,256,1024]{2,1,0:T(8,128)(2,1)} fusion(bf16[4,256,1024]{2,1,0:T(8,128)(2,1)} %bitcast.1, s32[1024]{0:T(1024)S(1)} %pad_clamp_fusion.2), kind=kCustom, calls=%fused_computation.clone | custom fusion | bytes 4194320 | tf_op jit(solution)/shard_map/jit(_take)/gather | solution.py:48
  43.1 1.9 broadcast_select_fusion.1
  45.0 1.2 dynamic-slice_bitcast_fusion.3
  46.1 5.0 %collective-permute-start = (bf16[1,256,1024]{2,1,0:T(8,128)(2,1)}, bf16[1,256,1024]{2,1,0:T(8,128)(2,1)S(1)}, u32[]{:S(2)}, u32[]{:S(2)}) collective-permute-start(bf16[1,256,1024]{2,1,0:T(8,128)(2,1)} %get-tuple-element.19), channel_id=1, source_target_pairs={{0,4},{4,8},{8,12},{12,16},{16,20},{20,24},{24,28},{28,32},{32,36}... | collective-permute-start | bytes 1572872 | tf_op jit(solution)/shard_map/ppermute | solution.py:12
  51.1 3.3 %collective-permute-start.1 = (bf16[1,256,1024]{2,1,0:T(8,128)(2,1)}, bf16[1,256,1024]{2,1,0:T(8,128)(2,1)}, u32[]{:S(2)}, u32[]{:S(2)}) collective-permute-start(bf16[1,256,1024]{2,1,0:T(8,128)(2,1)} %get-tuple-element.19), channel_id=1, source_target_pairs={{12,0},{16,4},{20,8},{24,12},{28,16},{32,20},{36,24},{40,28},{44,3... | collective-permute-start | bytes 1572872 | tf_op jit(solution)/shard_map/ppermute | solution.py:12
  54.5 0.1 select_reduce_fusion
  54.6 1.9 collective-permute-start.2
  56.5 5.5 %collective-permute-start.3 = (bf16[1,256,1024]{2,1,0:T(8,128)(2,1)}, bf16[1,256,1024]{2,1,0:T(8,128)(2,1)}, u32[]{:S(2)}, u32[]{:S(2)}) collective-permute-start(bf16[1,256,1024]{2,1,0:T(8,128)(2,1)} %get-tuple-element.18), channel_id=1, source_target_pairs={{8,0},{12,4},{16,8},{20,12},{24,16},{28,20},{32,24},{36,28},{40,32... | collective-permute-start | bytes 1572872 | tf_op jit(solution)/shard_map/ppermute | solution.py:12
  62.0 2.4 %collective-permute-start.4 = (bf16[1,256,1024]{2,1,0:T(8,128)(2,1)}, bf16[1,256,1024]{2,1,0:T(8,128)(2,1)S(1)}, u32[]{:S(2)}, u32[]{:S(2)}) collective-permute-start(bf16[1,256,1024]{2,1,0:T(8,128)(2,1)} %get-tuple-element.17), channel_id=1, source_target_pairs={{0,12},{4,16},{8,20},{12,24},{16,28},{20,32},{24,36},{28,40},{32,4... | collective-permute-start | bytes 1572872 | tf_op jit(solution)/shard_map/ppermute | solution.py:12
  64.4 0.0 collective-permute-done
  64.4 3.6 %collective-permute-start.5 = (bf16[1,256,1024]{2,1,0:T(8,128)(2,1)}, bf16[1,256,1024]{2,1,0:T(8,128)(2,1)S(1)}, u32[]{:S(2)}, u32[]{:S(2)}) collective-permute-start(bf16[1,256,1024]{2,1,0:T(8,128)(2,1)} %get-tuple-element.17), channel_id=1, source_target_pairs={{4,0},{8,4},{12,8},{16,12},{20,16},{24,20},{28,24},{32,28},{36,32}... | collective-permute-start | bytes 1572872 | tf_op jit(solution)/shard_map/ppermute | solution.py:12
  68.0 2.1 %collective-permute-done.1 = bf16[1,256,1024]{2,1,0:T(8,128)(2,1)} collective-permute-done((bf16[1,256,1024]{2,1,0:T(8,128)(2,1)}, bf16[1,256,1024]{2,1,0:T(8,128)(2,1)}, u32[]{:S(2)}, u32[]{:S(2)}) %collective-permute-start.1) | collective-permute-done | bytes 524320 | tf_op jit(solution)/shard_map/ppermute | solution.py:12
  70.1 0.1 select_bitcast_fusion.5
  70.2 11.1 %collective-permute-done.2 = bf16[1,256,1024]{2,1,0:T(8,128)(2,1)} collective-permute-done((bf16[1,256,1024]{2,1,0:T(8,128)(2,1)}, bf16[1,256,1024]{2,1,0:T(8,128)(2,1)}, u32[]{:S(2)}, u32[]{:S(2)}) %collective-permute-start.2) | collective-permute-done | bytes 524320 | tf_op jit(solution)/shard_map/ppermute | solution.py:12
  81.3 0.0 collective-permute-done.3
  81.3 1.1 select_bitcast_fusion.4
  82.4 10.4 %collective-permute-done.4 = bf16[1,256,1024]{2,1,0:T(8,128)(2,1)S(1)} collective-permute-done((bf16[1,256,1024]{2,1,0:T(8,128)(2,1)}, bf16[1,256,1024]{2,1,0:T(8,128)(2,1)S(1)}, u32[]{:S(2)}, u32[]{:S(2)}) %collective-permute-start.4) | collective-permute-done | bytes 524320 | tf_op jit(solution)/shard_map/ppermute | solution.py:12
  92.8 0.0 collective-permute-done.5
  92.8 0.1 select_bitcast_fusion.3
  92.8 1.6 maximum_bitcast_fusion
  94.4 3.6 %gather_fusion.1 = bf16[4,256,1024]{2,1,0:T(8,128)(2,1)} fusion(bf16[4,256,1024]{2,1,0:T(8,128)(2,1)} %maximum_bitcast_fusion, s32[1024]{0:T(1024)S(1)} %pad_clamp_fusion.1), kind=kCustom, calls=%fused_computation.1.clone | custom fusion | bytes 4194320 | tf_op jit(solution)/shard_map/jit(_take)/gather | solution.py:30
  98.0 4.3 %multiply_reduce_fusion.1 = (f32[]{:T(128)}, bf16[4,1,256,1024]{3,2,0,1:T(8,128)(2,1)}) fusion(bf16[4,256,1024]{2,1,0:T(8,128)(2,1)} %gather_fusion.1, pred[4]{0:T(512)(128)(4,1)S(1)} %get-tuple-element.23), kind=kLoop, calls=%fused_computation.8 | loop fusion | flops 4194303 | bytes 4194312 | tf_op jit(solution)/shard_map/reduce_sum | solution.py:64
  102.3 0.0 copy-done
  102.3 9.5 %multiply_reduce_fusion = (f32[]{:T(128)}, f32[1024,1024]{1,0:T(8,128)}) fusion(bf16[1,1024,1024]{2,1,0:T(8,128)(2,1)S(1)} %copy-done, bf16[1024,1024]{1,0:T(8,128)(2,1)} %bitcast.71, bf16[1,1024,1024]{2,1,0:T(8,128)(2,1)} %param.14), kind=kOutput, calls=%fused_computation.7 | convolution fusion | flops 4298113024 | bytes 10485764 | tf_op jit(solution)/shard_map/qab,qbc->qac/dot_general | solution.py:60
  113.2 2.8 %multiply_convert_fusion = bf16[1024,1024]{1,0:T(8,128)(2,1)S(1)} fusion(f32[1024,1024]{1,0:T(8,128)} %get-tuple-element.21, f32[]{:T(128)S(6)} %sqrt.4), kind=kLoop, calls=%fused_computation.6 | loop fusion | flops 2097152 | bytes 6291460 | tf_op jit(solution)/shard_map/convert_element_type | solution.py:68
  115.9 0.1 dynamic-slice_bitcast_fusion.2
  116.1 1.9 collective-permute-start.6
  118.0 3.2 %collective-permute-start.7 = (bf16[1,256,1024]{2,1,0:T(8,128)(2,1)S(1)}, bf16[1,256,1024]{2,1,0:T(8,128)(2,1)S(1)}, u32[]{:S(2)}, u32[]{:S(2)}) collective-permute-start(bf16[1,256,1024]{2,1,0:T(8,128)(2,1)S(1)} %get-tuple-element.13), channel_id=1, source_target_pairs={{12,0},{16,4},{20,8},{24,12},{28,16},{32,20},{36,24},{40,28},{44,3... | collective-permute-start | bytes 1572872 | tf_op jit(solution)/shard_map/ppermute | solution.py:12
  121.2 2.5 %collective-permute-start.8 = (bf16[1,256,1024]{2,1,0:T(8,128)(2,1)S(1)}, bf16[1,256,1024]{2,1,0:T(8,128)(2,1)S(1)}, u32[]{:S(2)}, u32[]{:S(2)}) collective-permute-start(bf16[1,256,1024]{2,1,0:T(8,128)(2,1)S(1)} %get-tuple-element.14), channel_id=1, source_target_pairs={{0,8},{4,12},{8,16},{12,20},{16,24},{20,28},{24,32},{28,36},{32,40... | collective-permute-start | bytes 1572872 | tf_op jit(solution)/shard_map/ppermute | solution.py:12
  123.7 4.9 %collective-permute-start.9 = (bf16[1,256,1024]{2,1,0:T(8,128)(2,1)S(1)}, bf16[1,256,1024]{2,1,0:T(8,128)(2,1)S(1)}, u32[]{:S(2)}, u32[]{:S(2)}) collective-permute-start(bf16[1,256,1024]{2,1,0:T(8,128)(2,1)S(1)} %get-tuple-element.14), channel_id=1, source_target_pairs={{8,0},{12,4},{16,8},{20,12},{24,16},{28,20},{32,24},{36,28},{40,32... | collective-permute-start | bytes 1572872 | tf_op jit(solution)/shard_map/ppermute | solution.py:12
  128.6 2.3 %collective-permute-start.10 = (bf16[1,256,1024]{2,1,0:T(8,128)(2,1)S(1)}, bf16[1,256,1024]{2,1,0:T(8,128)(2,1)S(1)}, u32[]{:S(2)}, u32[]{:S(2)}) collective-permute-start(bf16[1,256,1024]{2,1,0:T(8,128)(2,1)S(1)} %get-tuple-element.15), channel_id=1, source_target_pairs={{0,12},{4,16},{8,20},{12,24},{16,28},{20,32},{24,36},{28,40},{32,4... | collective-permute-start | bytes 1572872 | tf_op jit(solution)/shard_map/ppermute | solution.py:12
  131.0 0.0 collective-permute-done.6
  131.0 3.6 %collective-permute-start.11 = (bf16[1,256,1024]{2,1,0:T(8,128)(2,1)S(1)}, bf16[1,256,1024]{2,1,0:T(8,128)(2,1)S(1)}, u32[]{:S(2)}, u32[]{:S(2)}) collective-permute-start(bf16[1,256,1024]{2,1,0:T(8,128)(2,1)S(1)} %get-tuple-element.15), channel_id=1, source_target_pairs={{4,0},{8,4},{12,8},{16,12},{20,16},{24,20},{28,24},{32,28},{36,32}... | collective-permute-start | bytes 1572872 | tf_op jit(solution)/shard_map/ppermute | solution.py:12
  134.7 2.0 collective-permute-done.7
  136.7 0.1 select_bitcast_fusion.2
  136.7 8.7 %collective-permute-done.8 = bf16[1,256,1024]{2,1,0:T(8,128)(2,1)S(1)} collective-permute-done((bf16[1,256,1024]{2,1,0:T(8,128)(2,1)S(1)}, bf16[1,256,1024]{2,1,0:T(8,128)(2,1)S(1)}, u32[]{:S(2)}, u32[]{:S(2)}) %collective-permute-start.8) | collective-permute-done | bytes 524320 | tf_op jit(solution)/shard_map/ppermute | solution.py:12
  145.4 2.4 %collective-permute-done.9 = bf16[1,256,1024]{2,1,0:T(8,128)(2,1)S(1)} collective-permute-done((bf16[1,256,1024]{2,1,0:T(8,128)(2,1)S(1)}, bf16[1,256,1024]{2,1,0:T(8,128)(2,1)S(1)}, u32[]{:S(2)}, u32[]{:S(2)}) %collective-permute-start.9) | collective-permute-done | bytes 524320 | tf_op jit(solution)/shard_map/ppermute | solution.py:12
  147.8 0.1 select_bitcast_fusion.1
  147.9 9.8 %collective-permute-done.10 = bf16[1,256,1024]{2,1,0:T(8,128)(2,1)S(1)} collective-permute-done((bf16[1,256,1024]{2,1,0:T(8,128)(2,1)S(1)}, bf16[1,256,1024]{2,1,0:T(8,128)(2,1)S(1)}, u32[]{:S(2)}, u32[]{:S(2)}) %collective-permute-start.10) | collective-permute-done | bytes 524320 | tf_op jit(solution)/shard_map/ppermute | solution.py:12
  157.7 0.0 collective-permute-done.11
  157.7 0.1 select_bitcast_fusion
  157.7 0.3 maximum_bitcast_fusion.1
  158.0 2.0 gather_fusion.2
  160.0 3.2 %fusion.1 = bf16[4,256,1024]{2,1,0:T(8,128)(2,1)} fusion(bf16[4,256,1024]{2,1,0:T(8,128)(2,1)} %gather_fusion.2, pred[4]{0:T(512)(128)(4,1)S(1)} %get-tuple-element.23), kind=kLoop, calls=%fused_computation.13 | loop fusion | flops 1048576 | bytes 4194308 | tf_op jit(solution)/shard_map/reshape | solution.py:73
  163.2 2.3 %gather_fusion.3 = bf16[4,256,1024]{2,1,0:T(8,128)(2,1)S(1)} fusion(bf16[4,256,1024]{2,1,0:T(8,128)(2,1)} %fusion.1, s32[1024]{0:T(1024)S(1)} %pad_clamp_fusion), kind=kCustom, calls=%fused_computation.2.clone | custom fusion | bytes 4194320 | tf_op jit(solution)/shard_map/jit(_take)/gather | solution.py:78
  165.5 1.6 broadcast_select_fusion
  167.1 3.8 %all-to-all-start.1 = ((bf16[4,256,1024]{2,1,0:T(8,128)(2,1)}), bf16[4,256,1024]{2,1,0:T(8,128)(2,1)S(1)}, u32[]{:S(2)}, u32[]{:S(2)}) async-start(bf16[4,256,1024]{2,1,0:T(8,128)(2,1)} %broadcast_select_fusion), calls=%async_computation.1 | async-start | bytes 4194304 | tf_op jit(solution)/shard_map/all_to_all | solution.py:79
  170.9 0.0 copy-start.2
  170.9 0.0 copy-start.3
  170.9 8.0 %bitcast_add_fusion = f32[1,1024,1024]{2,1,0:T(8,128)} fusion(f32[1,1024,1024]{2,1,0:T(8,128)} %param.13, bf16[4,1,256,1024]{3,2,0,1:T(8,128)(2,1)} %get-tuple-element.12), kind=kOutput, calls=%fused_computation.4 | convolution fusion | flops 2148532224 | bytes 10485760 | tf_op jit(solution)/shard_map/qba,qbc->qac/dot_general | solution.py:54
  178.9 0.0 copy-done.2
  178.9 0.0 copy-done.3
  178.9 4.4 %bitcast_add_fusion.1 = f32[1,1024,1024]{2,1,0:T(8,128)} fusion(f32[1,1024,1024]{2,1,0:T(8,128)S(1)} %copy-done.3, bf16[1024,1024]{1,0:T(8,128)(2,1)S(1)} %bitcast.72), kind=kOutput, calls=%fused_computation.5 | convolution fusion | flops 2148532224 | bytes 10485760 | tf_op jit(solution)/shard_map/qab,qcb->qac/dot_general | solution.py:51
  183.3 13.9 %all-to-all-done.1 = bf16[4,256,1024]{2,1,0:T(8,128)(2,1)S(1)} async-done(((bf16[4,256,1024]{2,1,0:T(8,128)(2,1)}), bf16[4,256,1024]{2,1,0:T(8,128)(2,1)S(1)}, u32[]{:S(2)}, u32[]{:S(2)}) %all-to-all-start.1) | async-done | bytes 2097184 | tf_op jit(solution)/shard_map/all_to_all | solution.py:79
  197.1 2.5 %copy.24 = bf16[256,4,1024]{0,2,1:T(8,128)(2,1)} copy(bf16[256,4,1024]{2,0,1:T(8,128)(2,1)S(1)} %bitcast.68) | data formatting | bytes 4194304 | tf_op jit(solution)/shard_map/all_to_all | solution.py:79
  199.7 0.0 copy-start.1
  199.7 4.2 %copy.26 = bf16[256,4096]{1,0:T(8,128)(2,1)} copy(bf16[256,4096]{0,1:T(8,128)(2,1)} %bitcast.69) | data formatting | bytes 4194304
  203.9 0.0 copy-done.1
  (9 shorter events, 0.1 us)
Async XLA Ops:
  0.6 101.7 %copy-start = (bf16[1,1024,1024]{2,1,0:T(8,128)(2,1)S(1)}, bf16[1,1024,1024]{2,1,0:T(8,128)(2,1)}, u32[]{:S(2)}) copy-start(bf16[1,1024,1024]{2,1,0:T(8,128)(2,1)} %param.15) | copy-start | bytes 6291460
  8.8 30.7 %all-to-all-start = ((bf16[256,4,1024]{2,0,1:T(8,128)(2,1)}), bf16[256,4,1024]{2,0,1:T(8,128)(2,1)}, u32[]{:S(2)}, u32[]{:S(2)}) async-start(bf16[256,4,1024]{2,0,1:T(8,128)(2,1)} %copy.22), calls=%async_computation | async-start | bytes 4194304 | tf_op jit(solution)/shard_map/all_to_all | solution.py:45
  46.1 18.3 %collective-permute-start = (bf16[1,256,1024]{2,1,0:T(8,128)(2,1)}, bf16[1,256,1024]{2,1,0:T(8,128)(2,1)S(1)}, u32[]{:S(2)}, u32[]{:S(2)}) collective-permute-start(bf16[1,256,1024]{2,1,0:T(8,128)(2,1)} %get-tuple-element.19), channel_id=1, source_target_pairs={{0,4},{4,8},{8,12},{12,16},{16,20},{20,24},{24,28},{28,32},{32,36}... | collective-permute-start | bytes 1572872 | tf_op jit(solution)/shard_map/ppermute | solution.py:12
  51.1 19.0 %collective-permute-start.1 = (bf16[1,256,1024]{2,1,0:T(8,128)(2,1)}, bf16[1,256,1024]{2,1,0:T(8,128)(2,1)}, u32[]{:S(2)}, u32[]{:S(2)}) collective-permute-start(bf16[1,256,1024]{2,1,0:T(8,128)(2,1)} %get-tuple-element.19), channel_id=1, source_target_pairs={{12,0},{16,4},{20,8},{24,12},{28,16},{32,20},{36,24},{40,28},{44,3... | collective-permute-start | bytes 1572872 | tf_op jit(solution)/shard_map/ppermute | solution.py:12
  54.6 26.7 %collective-permute-start.2 = (bf16[1,256,1024]{2,1,0:T(8,128)(2,1)}, bf16[1,256,1024]{2,1,0:T(8,128)(2,1)}, u32[]{:S(2)}, u32[]{:S(2)}) collective-permute-start(bf16[1,256,1024]{2,1,0:T(8,128)(2,1)} %get-tuple-element.18), channel_id=1, source_target_pairs={{0,8},{4,12},{8,16},{12,20},{16,24},{20,28},{24,32},{28,36},{32,40... | collective-permute-start | bytes 1572872 | tf_op jit(solution)/shard_map/ppermute | solution.py:12
  56.5 24.8 %collective-permute-start.3 = (bf16[1,256,1024]{2,1,0:T(8,128)(2,1)}, bf16[1,256,1024]{2,1,0:T(8,128)(2,1)}, u32[]{:S(2)}, u32[]{:S(2)}) collective-permute-start(bf16[1,256,1024]{2,1,0:T(8,128)(2,1)} %get-tuple-element.18), channel_id=1, source_target_pairs={{8,0},{12,4},{16,8},{20,12},{24,16},{28,20},{32,24},{36,28},{40,32... | collective-permute-start | bytes 1572872 | tf_op jit(solution)/shard_map/ppermute | solution.py:12
  62.0 30.7 %collective-permute-start.4 = (bf16[1,256,1024]{2,1,0:T(8,128)(2,1)}, bf16[1,256,1024]{2,1,0:T(8,128)(2,1)S(1)}, u32[]{:S(2)}, u32[]{:S(2)}) collective-permute-start(bf16[1,256,1024]{2,1,0:T(8,128)(2,1)} %get-tuple-element.17), channel_id=1, source_target_pairs={{0,12},{4,16},{8,20},{12,24},{16,28},{20,32},{24,36},{28,40},{32,4... | collective-permute-start | bytes 1572872 | tf_op jit(solution)/shard_map/ppermute | solution.py:12
  64.4 28.4 %collective-permute-start.5 = (bf16[1,256,1024]{2,1,0:T(8,128)(2,1)}, bf16[1,256,1024]{2,1,0:T(8,128)(2,1)S(1)}, u32[]{:S(2)}, u32[]{:S(2)}) collective-permute-start(bf16[1,256,1024]{2,1,0:T(8,128)(2,1)} %get-tuple-element.17), channel_id=1, source_target_pairs={{4,0},{8,4},{12,8},{16,12},{20,16},{24,20},{28,24},{32,28},{36,32}... | collective-permute-start | bytes 1572872 | tf_op jit(solution)/shard_map/ppermute | solution.py:12
  116.1 14.9 %collective-permute-start.6 = (bf16[1,256,1024]{2,1,0:T(8,128)(2,1)S(1)}, bf16[1,256,1024]{2,1,0:T(8,128)(2,1)S(1)}, u32[]{:S(2)}, u32[]{:S(2)}) collective-permute-start(bf16[1,256,1024]{2,1,0:T(8,128)(2,1)S(1)} %get-tuple-element.13), channel_id=1, source_target_pairs={{0,4},{4,8},{8,12},{12,16},{16,20},{20,24},{24,28},{28,32},{32,36}... | collective-permute-start | bytes 1572872 | tf_op jit(solution)/shard_map/ppermute | solution.py:12
  118.0 18.7 %collective-permute-start.7 = (bf16[1,256,1024]{2,1,0:T(8,128)(2,1)S(1)}, bf16[1,256,1024]{2,1,0:T(8,128)(2,1)S(1)}, u32[]{:S(2)}, u32[]{:S(2)}) collective-permute-start(bf16[1,256,1024]{2,1,0:T(8,128)(2,1)S(1)} %get-tuple-element.13), channel_id=1, source_target_pairs={{12,0},{16,4},{20,8},{24,12},{28,16},{32,20},{36,24},{40,28},{44,3... | collective-permute-start | bytes 1572872 | tf_op jit(solution)/shard_map/ppermute | solution.py:12
  121.2 24.2 %collective-permute-start.8 = (bf16[1,256,1024]{2,1,0:T(8,128)(2,1)S(1)}, bf16[1,256,1024]{2,1,0:T(8,128)(2,1)S(1)}, u32[]{:S(2)}, u32[]{:S(2)}) collective-permute-start(bf16[1,256,1024]{2,1,0:T(8,128)(2,1)S(1)} %get-tuple-element.14), channel_id=1, source_target_pairs={{0,8},{4,12},{8,16},{12,20},{16,24},{20,28},{24,32},{28,36},{32,40... | collective-permute-start | bytes 1572872 | tf_op jit(solution)/shard_map/ppermute | solution.py:12
  123.7 24.1 %collective-permute-start.9 = (bf16[1,256,1024]{2,1,0:T(8,128)(2,1)S(1)}, bf16[1,256,1024]{2,1,0:T(8,128)(2,1)S(1)}, u32[]{:S(2)}, u32[]{:S(2)}) collective-permute-start(bf16[1,256,1024]{2,1,0:T(8,128)(2,1)S(1)} %get-tuple-element.14), channel_id=1, source_target_pairs={{8,0},{12,4},{16,8},{20,12},{24,16},{28,20},{32,24},{36,28},{40,32... | collective-permute-start | bytes 1572872 | tf_op jit(solution)/shard_map/ppermute | solution.py:12
  128.6 29.1 %collective-permute-start.10 = (bf16[1,256,1024]{2,1,0:T(8,128)(2,1)S(1)}, bf16[1,256,1024]{2,1,0:T(8,128)(2,1)S(1)}, u32[]{:S(2)}, u32[]{:S(2)}) collective-permute-start(bf16[1,256,1024]{2,1,0:T(8,128)(2,1)S(1)} %get-tuple-element.15), channel_id=1, source_target_pairs={{0,12},{4,16},{8,20},{12,24},{16,28},{20,32},{24,36},{28,40},{32,4... | collective-permute-start | bytes 1572872 | tf_op jit(solution)/shard_map/ppermute | solution.py:12
  131.0 26.7 %collective-permute-start.11 = (bf16[1,256,1024]{2,1,0:T(8,128)(2,1)S(1)}, bf16[1,256,1024]{2,1,0:T(8,128)(2,1)S(1)}, u32[]{:S(2)}, u32[]{:S(2)}) collective-permute-start(bf16[1,256,1024]{2,1,0:T(8,128)(2,1)S(1)} %get-tuple-element.15), channel_id=1, source_target_pairs={{4,0},{8,4},{12,8},{16,12},{20,16},{24,20},{28,24},{32,28},{36,32}... | collective-permute-start | bytes 1572872 | tf_op jit(solution)/shard_map/ppermute | solution.py:12
  167.1 30.1 %all-to-all-start.1 = ((bf16[4,256,1024]{2,1,0:T(8,128)(2,1)}), bf16[4,256,1024]{2,1,0:T(8,128)(2,1)S(1)}, u32[]{:S(2)}, u32[]{:S(2)}) async-start(bf16[4,256,1024]{2,1,0:T(8,128)(2,1)} %broadcast_select_fusion), calls=%async_computation.1 | async-start | bytes 4194304 | tf_op jit(solution)/shard_map/all_to_all | solution.py:79
  170.9 8.0 %copy-start.2 = (bf16[4,1,256,1024]{3,2,0,1:T(8,128)(2,1)S(1)}, bf16[4,1,256,1024]{3,2,0,1:T(8,128)(2,1)}, u32[]{:S(2)}) copy-start(bf16[4,1,256,1024]{3,2,0,1:T(8,128)(2,1)} %get-tuple-element.12) | copy-start | bytes 6291460
  170.9 8.0 %copy-start.3 = (f32[1,1024,1024]{2,1,0:T(8,128)S(1)}, f32[1,1024,1024]{2,1,0:T(8,128)}, u32[]{:S(2)}) copy-start(f32[1,1024,1024]{2,1,0:T(8,128)} %param.12) | copy-start | bytes 12582916
  199.7 4.2 %copy-start.1 = (bf16[1,1024,1024]{2,1,0:T(8,128)(2,1)S(1)}, bf16[1,1024,1024]{2,1,0:T(8,128)(2,1)}, u32[]{:S(2)}) copy-start(bf16[1,1024,1024]{2,1,0:T(8,128)(2,1)} %param.15) | copy-start | bytes 6291460
where the time goes:
time: 205 us; the launch traced here: 204 us
  waiting for transfers between devices  85.1 us (42%)
  starting transfers between devices  48.9 us (24%)
  local copies, waits for them, and re-layouts  28.6 us (14%)
  matrix products  21.9 us (11%)
  other arithmetic  17.1 us (8%)
  between operations  2.2 us (1%)
    ppermute x12, waiting for transfers between devices, shifted(): lax.ppermute(value, axis, [(source, source + steps) for source in range(f...  46.5 us
    ppermute x12, starting transfers between devices, shifted(): lax.ppermute(value, axis, [(source, source + steps) for source in range(f...  40.1 us
    all_to_all x1, waiting for transfers between devices, per_device(): lax.all_to_all(gradient, 'tensor', split_axis=1, concat_axis=0, tiled=True)  24.8 us
    all_to_all x1, waiting for transfers between devices, per_device(): lax.all_to_all(by_slot, 'tensor', split_axis=0, concat_axis=1, tiled=True)  13.9 us
    dot_general x1, matrix products, per_device(): jnp.einsum('qab,qbc->qac', half_product, right_root, preferred_element_ty...  9.52 us
    unnamed x10, local copies, waits for them, and re-layouts  8.46 us
    dot_general x1, matrix products, per_device(): jnp.einsum('qba,qbc->qac', blocks, blocks, preferred_element_type=jnp.flo...  8 us
    gather x2, local copies, waits for them, and re-layouts, route_direct(): jnp.take(stacked, (member - jnp.arange(group_size)) % group_size, axis=0)  5.59 us
  transfers between devices with their start and end apart: 14, of which 9 were waited for; matrix products, arithmetic and copies ran while one was open for 7% of the time, Pallas kernels for 0%

commit v1 on v0

v1 whole, which is shorter than its diff:
```python
import jax
import jax.numpy as jnp
from jax import lax
from jax.experimental import pallas as pl
from jax.experimental.pallas import tpu as pltpu
from jax.sharding import PartitionSpec as P

B = 1024
GROUP = 4
TENSORS = 4
ROWS = B // GROUP
W = 128
CHUNKS = B // W
PANEL = 256
AHEAD = 3
MESH = pl.DeviceIdType.MESH


def fold(x):
    return jnp.sum(x.reshape(-1, 8, 128), axis=0)


def kernel(slot, grad, lf, rf, lroot, rroot, upd, nl, nr, *scratch):
    scratch = list(scratch)
    take = lambda n: [scratch.pop(0) for _ in range(n)]
    zr, yst, yr, zst = take(CHUNKS), take(CHUNKS), take(CHUNKS), take(CHUNKS)
    g, gt, half, pst, lv, rv, gsq, psq, sc_out, sc_in = take(10)
    load_sem, own_sem, z_send, z_recv, y_send, y_recv = take(6)
    by_send, by_recv, sc_send, sc_recv, bz_send, bz_recv = take(6)

    dp, z = lax.axis_index("dp"), lax.axis_index("tensor")
    m = lax.rem(dp, GROUP)
    base = dp - m
    row_block = lax.div(dp, GROUP)
    z_peers = [lax.rem(z + o, TENSORS) for o in range(TENSORS)]
    m_peers = [lax.rem(m + o, GROUP) for o in range(GROUP)]
    z_dev = [(dp, t) for t in z_peers]
    m_dev = [(base + q, z) for q in m_peers]

    loads = [
        pltpu.make_async_copy(src, dst, load_sem.at[i])
        for i, (src, dst) in enumerate(
            [(lroot.at[0], lv), (rroot.at[0], rv), (lf.at[0], nl), (rf.at[0], nr)]
        )
    ]

    def own_copy(c):
        return pltpu.make_async_copy(
            grad.at[:, pl.ds(pl.multiple_of(z * B + c * W, W), W)], zr[c].at[z], own_sem.at[c]
        )

    def z_copy(c, o):
        return pltpu.make_async_remote_copy(
            src_ref=grad.at[:, pl.ds(pl.multiple_of(z_peers[o] * B + c * W, W), W)],
            dst_ref=zr[c].at[z],
            send_sem=z_send.at[c, o],
            recv_sem=z_recv.at[c, o],
            device_id=z_dev[o],
            device_id_type=MESH,
        )

    def y_copy(c, o):
        return pltpu.make_async_remote_copy(
            src_ref=yst[c].at[o - 1],
            dst_ref=g.at[pl.ds(pl.multiple_of(m * ROWS, ROWS), ROWS), pl.ds(c * W, W)],
            send_sem=y_send.at[c, o],
            recv_sem=y_recv.at[c, o],
            device_id=m_dev[o],
            device_id_type=MESH,
        )

    def by_copy(c, o):
        return pltpu.make_async_remote_copy(
            src_ref=pst.at[pl.ds(pl.multiple_of(m_peers[o] * ROWS, ROWS), ROWS), pl.ds(c * W, W)],
            dst_ref=yr[c].at[m],
            send_sem=by_send.at[c, o],
            recv_sem=by_recv.at[c, o],
            device_id=m_dev[o],
            device_id_type=MESH,
        )

    def sc_copy(o):
        return pltpu.make_async_remote_copy(
            src_ref=sc_out,
            dst_ref=sc_in.at[m],
            send_sem=sc_send.at[o],
            recv_sem=sc_recv.at[o],
            device_id=m_dev[o],
            device_id_type=MESH,
        )

    def bz_copy(c, o):
        return pltpu.make_async_remote_copy(
            src_ref=zst[c].at[o - 1],
            dst_ref=upd.at[z, :, pl.ds(c * W, W)],
            send_sem=bz_send.at[c, o],
            recv_sem=bz_recv.at[c, o],
            device_id=z_dev[o],
            device_id_type=MESH,
        )

    others = (1, 3, 2)

    def send_z(c):
        for o in others:
            z_copy(c, o).start()
        own_copy(c).start()

    barrier = pltpu.get_barrier_semaphore()
    for o in range(1, TENSORS):
        pl.semaphore_signal(barrier, inc=1, device_id=z_dev[o], device_id_type=MESH)
    for o in range(1, GROUP):
        pl.semaphore_signal(barrier, inc=1, device_id=m_dev[o], device_id_type=MESH)
    pl.semaphore_wait(barrier, TENSORS + GROUP - 2)

    for c in range(AHEAD):
        send_z(c)
    for copy in loads:
        copy.start()

    gsq[...] = jnp.zeros_like(gsq)
    psq[...] = jnp.zeros_like(psq)
    mine = pl.ds(pl.multiple_of(m * ROWS, ROWS), ROWS)

    def relay(c):
        own_copy(c).wait()
        for o in others:
            z_copy(c, o).wait_recv()
        for o in (1, 2, 3):
            yst[c][o - 1] = zr[c][slot[row_block, z, m_peers[o]]]
            y_copy(c, o).start()
        g[mine, pl.ds(c * W, W)] = zr[c][slot[row_block, z, m]]

    def left_product(c):
        for o in (1, 2, 3):
            y_copy(c, o).wait_recv()
        cols = pl.ds(c * W, W)

        @pl.loop(0, B, step=PANEL)
        def _(r):
            rows = pl.ds(pl.multiple_of(r, PANEL), PANEL)
            part = g[rows, cols].astype(jnp.float32)
            gsq[...] += fold(part * part)
            half[rows, cols] = jnp.dot(
                lv[rows, :], g[:, cols], preferred_element_type=jnp.float32
            ).astype(jnp.bfloat16)

    for c in range(CHUNKS):
        relay(c)
        if c + AHEAD < CHUNKS:
            send_z(c + AHEAD)
        if c == 1:
            loads[0].wait()
        if c >= 2:
            left_product(c - 2)
    loads[1].wait()
    left_product(CHUNKS - 2)
    left_product(CHUNKS - 1)

    def right_product(p):
        cols = pl.ds(p * PANEL, PANEL)

        @pl.loop(0, B, step=PANEL)
        def _(r):
            rows = pl.ds(pl.multiple_of(r, PANEL), PANEL)
            part = jnp.dot(half[rows, :], rv[:, cols], preferred_element_type=jnp.float32)
            square = part * part
            psq[...] += fold(square[:, :128]) + fold(square[:, 128:])
            pst[rows, cols] = part.astype(jnp.bfloat16)

    def send_back(c):
        for o in (1, 2, 3):
            by_copy(c, o).start()
        yr[c][m] = pst[mine, pl.ds(c * W, W)]

    right_product(0)
    send_back(0)
    for p in range(1, B // PANEL):
        right_product(p)
    count = 1.0 / (B * B)
    grad_mean = jnp.sum(gsq[...], axis=(0, 1), keepdims=True) * count
    pre_mean = jnp.sum(psq[...], axis=(0, 1), keepdims=True) * count
    scale = jnp.broadcast_to(jnp.sqrt(grad_mean / (pre_mean + 1e-6)), (8, 128))
    sc_out[...] = scale
    sc_in[m] = scale
    for o in (1, 2, 3):
        sc_copy(o).start()
    for c in range(1, CHUNKS):
        send_back(c)

    def left_gram(p):
        cols = pl.ds(p * PANEL, PANEL)

        @pl.loop(0, B, step=PANEL)
        def _(r):
            rows = pl.ds(pl.multiple_of(r, PANEL), PANEL)
            nl[rows, cols] += lax.dot_general(
                g[rows, :], g[cols, :], (((1,), (1,)), ((), ())), preferred_element_type=jnp.float32
            )

    def right_gram(p):
        cols = pl.ds(p * PANEL, PANEL)

        @pl.loop(0, B, step=PANEL)
        def _(r):
            rows = pl.ds(pl.multiple_of(r, PANEL), PANEL)
            nr[rows, cols] += jnp.dot(gt[rows, :], g[:, cols], preferred_element_type=jnp.float32)

    loads[2].wait()
    loads[3].wait()

    @pl.loop(0, B, step=PANEL)
    def _(r):
        rows = pl.ds(pl.multiple_of(r, PANEL), PANEL)
        gt[rows, :] = g[:, rows].T

    slots = [slot[row_block, z, q] for q in range(GROUP)]

    def relay_back(c):
        for o in (1, 2, 3):
            by_copy(c, o).wait_recv()
        for o in (1, 3, 2, 0):
            t = z_peers[o]
            q = jnp.int32(0)
            for other in range(1, GROUP):
                q = jnp.where(slots[other] == t, other, q)
            piece = (yr[c][q].astype(jnp.float32) * sc_in[q][0:1, :]).astype(jnp.bfloat16)
            if o:
                zst[c][o - 1] = piece
                bz_copy(c, o).start()
            else:
                upd[z, :, pl.ds(c * W, W)] = piece

    for c in range(CHUNKS):
        if c == 0:
            for o in (1, 2, 3):
                sc_copy(o).wait_recv()
        relay_back(c)
        if c < 4:
            left_gram(c)
        else:
            right_gram(c - 4)

    for c in range(CHUNKS):
        for o in (1, 2, 3):
            z_copy(c, o).wait_send()
            y_copy(c, o).wait_send()
            by_copy(c, o).wait_send()
            bz_copy(c, o).wait_send()
    for o in (1, 2, 3):
        sc_copy(o).wait_send()
    for c in range(CHUNKS):
        for o in (1, 2, 3):
            bz_copy(c, o).wait_recv()


def write_out(upd, nl, nr, update, new_left, new_right, sem):
    copies = [
        (upd.at[e], update.at[:, pl.ds(e * B, B)]) for e in range(TENSORS)
    ]
    for i in range(4):
        rows = pl.ds(i * ROWS, ROWS)
        copies.append((nl.at[rows], new_left.at[0, rows]))
        copies.append((nr.at[rows], new_right.at[0, rows]))
    copies = [pltpu.make_async_copy(a, b, sem.at[i]) for i, (a, b) in enumerate(copies)]
    for copy in copies:
        copy.start()
    for copy in copies:
        copy.wait()


def per_device(gradient, block_slot, left_factor, right_factor, left_root, right_root):
    vmem, hbm = pl.BlockSpec(memory_space=pltpu.VMEM), pl.BlockSpec(memory_space=pltpu.HBM)
    smem = pl.BlockSpec(memory_space=pltpu.SMEM)
    bf16, f32 = jnp.bfloat16, jnp.float32
    dma = pltpu.SemaphoreType.DMA
    parts = pl.pallas_call(
        kernel,
        out_shape=(
            pltpu.VMEM((TENSORS, ROWS, B), bf16),
            pltpu.VMEM((B, B), f32),
            pltpu.VMEM((B, B), f32),
        ),
        in_specs=[smem, hbm, hbm, hbm, hbm, hbm],
        out_specs=(vmem, vmem, vmem),
        scratch_shapes=[pltpu.VMEM((4, ROWS, W), bf16)] * CHUNKS
        + [pltpu.VMEM((3, ROWS, W), bf16)] * CHUNKS
        + [pltpu.VMEM((4, ROWS, W), bf16)] * CHUNKS
        + [pltpu.VMEM((3, ROWS, W), bf16)] * CHUNKS
        + [pltpu.VMEM((B, B), bf16)] * 6
        + [pltpu.VMEM((8, 128), f32)] * 3
        + [pltpu.VMEM((4, 8, 128), f32)]
        + [dma((4,)), dma((CHUNKS,))]
        + [dma((CHUNKS, 4))] * 6
        + [dma((4,))] * 2
        + [dma((CHUNKS, 4))] * 2,
        compiler_params=pltpu.CompilerParams(
            collective_id=0, has_side_effects=True, vmem_limit_bytes=32 * 2**20
        ),
        name="shampoo",
    )(
        block_slot,
        *[
            pltpu.with_memory_space_constraint(x, pltpu.HBM)
            for x in (gradient, left_factor, right_factor, left_root, right_root)
        ],
    )
    return pl.pallas_call(
        write_out,
        out_shape=(
            pltpu.HBM((ROWS, TENSORS * B), bf16),
            pltpu.HBM((1, B, B), f32),
            pltpu.HBM((1, B, B), f32),
        ),
        in_specs=[vmem] * 3,
        out_specs=[hbm] * 3,
        scratch_shapes=[dma((12,))],
        compiler_params=pltpu.CompilerParams(vmem_limit_bytes=2**20),
        name="write_out",
    )(*[pltpu.with_memory_space_constraint(x, pltpu.VMEM) for x in parts])


def solution(mesh):
    owned = P(("dp", "tensor"), None, None)
    return jax.shard_map(
        per_device,
        mesh=mesh,
        in_specs=(P("dp", "tensor"), P(), owned, owned, owned, owned),
        out_specs=(P("dp", "tensor"), owned, owned),
        check_vma=False,
    )
```

time: 205 us -> 77.8 us (0.38)
  waiting for transfers between devices: 85.1 us -> 0 us
  Pallas kernels: 0 us -> 75.4 us
  starting transfers between devices: 48.9 us -> 0 us
  local copies, waits for them, and re-layouts: 28.6 us -> 0.8 us
  matrix products: 21.9 us -> 0 us
  other arithmetic: 17.1 us -> 0 us
    pallas_call x0 -> x2, Pallas kernels: none -> 75.4 us  [the longest x1 71.3 us: per_device(): pl.pallas_call(kernel, out_shape=(pltpu.VMEM((TENSORS, ROWS, B), bf16), p...]
    ppermute x12 -> x0, waiting for transfers between devices: 46.5 us -> none  [shifted(): lax.ppermute(value, axis, [(source, source + steps) for source in range(f...]
    ppermute x12 -> x0, starting transfers between devices: 40.1 us -> none  [shifted(): lax.ppermute(value, axis, [(source, source + steps) for source in range(f...]
    all_to_all x2 -> x0, waiting for transfers between devices: 38.6 us -> none  [the longest x1 24.8 us: per_device(): lax.all_to_all(gradient, 'tensor', split_axis=1, concat_axis=0, tiled=True)]
    dot_general x3 -> x0, matrix products: 21.9 us -> none  [the longest x1 9.52 us: per_device(): jnp.einsum('qab,qbc->qac', half_product, right_root, preferred_element_ty...]
    gather x4 -> x0, local copies, waits for them, and re-layouts: 11.4 us -> none  [the longest x2 5.59 us: route_direct(): jnp.take(stacked, (member - jnp.arange(group_size)) % group_size, axis=0)]
    all_to_all x2 -> x0, starting transfers between devices: 8.81 us -> none  [the longest x1 5.03 us: per_device(): lax.all_to_all(gradient, 'tensor', split_axis=1, concat_axis=0, tiled=True)]
    unnamed x10 -> x1, local copies, waits for them, and re-layouts: 8.46 us -> 0.8 us
  transfers between devices with their start and end apart: 14 -> 0, of which waited for: 9 -> 0; matrix products, arithmetic and copies ran while one was open for 7% -> 0% of each run, Pallas kernels for 0% -> 0%
where the time goes in v1:
time: 77.8 us; the launch traced here: 76.8 us
  Pallas kernels  75.4 us (97%)
  local copies, waits for them, and re-layouts  0.8 us (1%)
    pallas_call x1, Pallas kernels, per_device(): pl.pallas_call(kernel, out_shape=(pltpu.VMEM((TENSORS, ROWS, B), bf16), p...  71.3 us
    pallas_call x1, Pallas kernels, per_device(): pl.pallas_call(write_out, out_shape=(pltpu.HBM((ROWS, TENSORS * B), bf16)...  4.04 us

profile of v1, /device:TPU:3, one launch (start us, length us, event | category | flops | bytes accessed | tf_op | source)
XLA Modules:
  0.0 76.8 jit_solution(155110844246210564)
XLA Ops:
  0.6 0.8 %copy.9.slot = s32[8,4,4]{2,1,0:T(4,128)S(1)} copy(s32[8,4,4]{0,2,1:T(4,128)} %param.7) | data formatting | bytes 1024 | tf_op args[1]
  1.4 71.3 %shampoo.1 = (bf16[4,256,1024]{2,1,0:T(8,128)(2,1)S(1)}, f32[1024,1024]{1,0:T(8,128)S(1)}, f32[1024,1024]{1,0:T(8,128)S(1)}) custom-call(s32[8,4,4]{2,1,0:T(4,128)S(1)} %copy.9.slot, bf16[256,4096]{1,0:T(8,128)(2,1)} %grad.1, f32[1,1024,1024]{2,1,0:T(8,128)} %lf.1, f32[1,1024,1024]{2,1,0:T(8,128)} %rf.1, bf16[1,1024,1024]{2,1,0:T(8,128)(2,1)} %lroot.1, ...), custom_call_target="tpu_custom_call" | custom-call | tf_op jit(solution)/shard_map/shampoo/pallas_call | solution.py:277
  72.8 4.0 %write_out.1 = (bf16[256,4096]{1,0:T(8,128)(2,1)}, f32[1,1024,1024]{2,1,0:T(8,128)}, f32[1,1024,1024]{2,1,0:T(8,128)}) custom-call(bf16[4,256,1024]{2,1,0:T(8,128)(2,1)S(1)} %get-tuple-element.6.upd, f32[1024,1024]{1,0:T(8,128)S(1)} %get-tuple-element.7.nl, f32[1024,1024]{1,0:T(8,128)S(1)} %get-tuple-element.8.nr), custom_call_target="tpu_custom_call" | custom-call | tf_op jit(solution)/shard_map/write_out/pallas_call | solution.py:308

commit v2 on v1

--- a/solution.py
+++ b/solution.py
@@ -20,11 +20,12 @@
     return jnp.sum(x.reshape(-1, 8, 128), axis=0)
 
 
-def kernel(slot, grad, lf, rf, lroot, rroot, upd, nl, nr, *scratch):
+def kernel(slot_hbm, grad, lf, rf, lroot, rroot, upd, nl, nr, *scratch):
     scratch = list(scratch)
     take = lambda n: [scratch.pop(0) for _ in range(n)]
     zr, yst, yr, zst = take(CHUNKS), take(CHUNKS), take(CHUNKS), take(CHUNKS)
     g, gt, half, pst, lv, rv, gsq, psq, sc_out, sc_in = take(10)
+    slot, slot_sem, acc = take(3)
     load_sem, own_sem, z_send, z_recv, y_send, y_recv = take(6)
     by_send, by_recv, sc_send, sc_recv, bz_send, bz_recv = take(6)
 
@@ -99,13 +100,15 @@
             device_id_type=MESH,
         )
 
-    others = (1, 3, 2)
+    others = (2, 1, 3)
 
     def send_z(c):
         for o in others:
             z_copy(c, o).start()
         own_copy(c).start()
 
+    slot_copy = pltpu.make_async_copy(slot_hbm, slot, slot_sem)
+    slot_copy.start()
     barrier = pltpu.get_barrier_semaphore()
     for o in range(1, TENSORS):
         pl.semaphore_signal(barrier, inc=1, device_id=z_dev[o], device_id_type=MESH)
@@ -117,6 +120,7 @@
         send_z(c)
     for copy in loads:
         copy.start()
+    slot_copy.wait()
 
     gsq[...] = jnp.zeros_like(gsq)
     psq[...] = jnp.zeros_like(psq)
@@ -127,16 +131,16 @@
         for o in others:
             z_copy(c, o).wait_recv()
         for o in (1, 2, 3):
-            yst[c][o - 1] = zr[c][slot[row_block, z, m_peers[o]]]
+            yst[c][o - 1] = zr[c][slot[z, m_peers[o], row_block]]
             y_copy(c, o).start()
-        g[mine, pl.ds(c * W, W)] = zr[c][slot[row_block, z, m]]
+        g[mine, pl.ds(c * W, W)] = zr[c][slot[z, m, row_block]]
 
     def left_product(c):
         for o in (1, 2, 3):
             y_copy(c, o).wait_recv()
         cols = pl.ds(c * W, W)
 
-        @pl.loop(0, B, step=PANEL)
+        @pl.loop(0, B, step=PANEL, unroll=True)
         def _(r):
             rows = pl.ds(pl.multiple_of(r, PANEL), PANEL)
             part = g[rows, cols].astype(jnp.float32)
@@ -144,6 +148,15 @@
             half[rows, cols] = jnp.dot(
                 lv[rows, :], g[:, cols], preferred_element_type=jnp.float32
             ).astype(jnp.bfloat16)
+
+    def partial_right(start, stop):
+        inner = pl.ds(start * W, (stop - start) * W)
+
+        @pl.loop(0, B, step=PANEL, unroll=True)
+        def _(r):
+            rows = pl.ds(pl.multiple_of(r, PANEL), PANEL)
+            part = jnp.dot(half[rows, inner], rv[inner, :], preferred_element_type=jnp.float32)
+            acc[rows, :] = part if start == 0 else acc[rows, :] + part
 
     for c in range(CHUNKS):
         relay(c)
@@ -153,17 +166,27 @@
             loads[0].wait()
         if c >= 2:
             left_product(c - 2)
-    loads[1].wait()
+        if c == 4:
+            loads[1].wait()
+            partial_right(0, 2)
+        if c == 6:
+            partial_right(2, 4)
+    partial_right(4, 6)
     left_product(CHUNKS - 2)
+    partial_right(6, 7)
     left_product(CHUNKS - 1)
+
+    inner = pl.ds(7 * W, W)
 
     def right_product(p):
         cols = pl.ds(p * PANEL, PANEL)
 
-        @pl.loop(0, B, step=PANEL)
-        def _(r):
-            rows = pl.ds(pl.multiple_of(r, PANEL), PANEL)
-            part = jnp.dot(half[rows, :], rv[:, cols], preferred_element_type=jnp.float32)
+        @pl.loop(0, B, step=PANEL, unroll=True)
+        def _(r):
+            rows = pl.ds(pl.multiple_of(r, PANEL), PANEL)
+            part = acc[rows, cols] + jnp.dot(
+                half[rows, inner], rv[inner, cols], preferred_element_type=jnp.float32
+            )
             square = part * part
             psq[...] += fold(square[:, :128]) + fold(square[:, 128:])
             pst[rows, cols] = part.astype(jnp.bfloat16)
@@ -191,7 +214,7 @@
     def left_gram(p):
         cols = pl.ds(p * PANEL, PANEL)
 
-        @pl.loop(0, B, step=PANEL)
+        @pl.loop(0, B, step=PANEL, unroll=True)
         def _(r):
             rows = pl.ds(pl.multiple_of(r, PANEL), PANEL)
             nl[rows, cols] += lax.dot_general(
@@ -201,7 +224,7 @@
     def right_gram(p):
         cols = pl.ds(p * PANEL, PANEL)
 
-        @pl.loop(0, B, step=PANEL)
+        @pl.loop(0, B, step=PANEL, unroll=True)
         def _(r):
             rows = pl.ds(pl.multiple_of(r, PANEL), PANEL)
             nr[rows, cols] += jnp.dot(gt[rows, :], g[:, cols], preferred_element_type=jnp.float32)
@@ -209,17 +232,17 @@
     loads[2].wait()
     loads[3].wait()
 
-    @pl.loop(0, B, step=PANEL)
+    @pl.loop(0, B, step=PANEL, unroll=True)
     def _(r):
         rows = pl.ds(pl.multiple_of(r, PANEL), PANEL)
         gt[rows, :] = g[:, rows].T
 
-    slots = [slot[row_block, z, q] for q in range(GROUP)]
+    slots = [slot[z, q, row_block] for q in range(GROUP)]
 
     def relay_back(c):
         for o in (1, 2, 3):
             by_copy(c, o).wait_recv()
-        for o in (1, 3, 2, 0):
+        for o in (2, 1, 3, 0):
             t = z_peers[o]
             q = jnp.int32(0)
             for other in range(1, GROUP):
@@ -231,27 +254,25 @@
             else:
                 upd[z, :, pl.ds(c * W, W)] = piece
 
+    for o in (1, 2, 3):
+        sc_copy(o).wait_recv()
     for c in range(CHUNKS):
-        if c == 0:
-            for o in (1, 2, 3):
-                sc_copy(o).wait_recv()
         relay_back(c)
         if c < 4:
             left_gram(c)
         else:
             right_gram(c - 4)
-
-    for c in range(CHUNKS):
         for o in (1, 2, 3):
             z_copy(c, o).wait_send()
             y_copy(c, o).wait_send()
-            by_copy(c, o).wait_send()
-            bz_copy(c, o).wait_send()
+            if c:
+                by_copy(c - 1, o).wait_send()
     for o in (1, 2, 3):
         sc_copy(o).wait_send()
+        by_copy(CHUNKS - 1, o).wait_send()
     for c in range(CHUNKS):
         for o in (1, 2, 3):
-            bz_copy(c, o).wait_recv()
+            bz_copy(c, o).wait()
 
 
 def write_out(upd, nl, nr, update, new_left, new_right, sem):
@@ -271,7 +292,6 @@
 
 def per_device(gradient, block_slot, left_factor, right_factor, left_root, right_root):
     vmem, hbm = pl.BlockSpec(memory_space=pltpu.VMEM), pl.BlockSpec(memory_space=pltpu.HBM)
-    smem = pl.BlockSpec(memory_space=pltpu.SMEM)
     bf16, f32 = jnp.bfloat16, jnp.float32
     dma = pltpu.SemaphoreType.DMA
     parts = pl.pallas_call(
@@ -281,7 +301,7 @@
             pltpu.VMEM((B, B), f32),
             pltpu.VMEM((B, B), f32),
         ),
-        in_specs=[smem, hbm, hbm, hbm, hbm, hbm],
+        in_specs=[hbm, hbm, hbm, hbm, hbm, hbm],
         out_specs=(vmem, vmem, vmem),
         scratch_shapes=[pltpu.VMEM((4, ROWS, W), bf16)] * CHUNKS
         + [pltpu.VMEM((3, ROWS, W), bf16)] * CHUNKS
@@ -290,6 +310,8 @@
         + [pltpu.VMEM((B, B), bf16)] * 6
         + [pltpu.VMEM((8, 128), f32)] * 3
         + [pltpu.VMEM((4, 8, 128), f32)]
+        + [pltpu.SMEM((TENSORS, GROUP, block_slot.shape[0]), jnp.int32), dma]
+        + [pltpu.VMEM((B, B), f32)]
         + [dma((4,)), dma((CHUNKS,))]
         + [dma((CHUNKS, 4))] * 6
         + [dma((4,))] * 2
@@ -299,10 +321,9 @@
         ),
         name="shampoo",
     )(
-        block_slot,
         *[
             pltpu.with_memory_space_constraint(x, pltpu.HBM)
-            for x in (gradient, left_factor, right_factor, left_root, right_root)
+            for x in (block_slot.transpose(1, 2, 0), gradient, left_factor, right_factor, left_root, right_root)
         ],
     )
     return pl.pallas_call(

time: 77.8 us -> 73.3 us (0.942)
  Pallas kernels: 75.4 us -> 71.5 us
  local copies, waits for them, and re-layouts: 0.8 us -> 0 us
    pallas_call x1, Pallas kernels: 71.3 us -> 67.5 us  [per_device(): pl.pallas_call(kernel, out_shape=(pltpu.VMEM((TENSORS, ROWS, B), bf16), p...]
    unnamed x1 -> x0, local copies, waits for them, and re-layouts: 0.8 us -> none
where the time goes in v2:
time: 73.3 us; the launch traced here: 72.3 us
  Pallas kernels  71.5 us (98%)
  between operations  0.8 us (1%)
    pallas_call x1, Pallas kernels, per_device(): pl.pallas_call(kernel, out_shape=(pltpu.VMEM((TENSORS, ROWS, B), bf16), p...  67.5 us
    pallas_call x1, Pallas kernels, per_device(): pl.pallas_call(write_out, out_shape=(pltpu.HBM((ROWS, TENSORS * B), bf16)...  4.04 us

profile of v2, /device:TPU:3, one launch (start us, length us, event | category | flops | bytes accessed | tf_op | source)
XLA Modules:
  0.0 72.3 jit_solution(299834231269301894)
XLA Ops:
  0.6 67.5 %shampoo.1 = (bf16[4,256,1024]{2,1,0:T(8,128)(2,1)S(1)}, f32[1024,1024]{1,0:T(8,128)S(1)}, f32[1024,1024]{1,0:T(8,128)S(1)}) custom-call(s32[4,4,8]{2,1,0:T(4,128)} %bitcast.1, bf16[256,4096]{1,0:T(8,128)(2,1)} %grad.1, f32[1,1024,1024]{2,1,0:T(8,128)} %lf.1, f32[1,1024,1024]{2,1,0:T(8,128)} %rf.1, bf16[1,1024,1024]{2,1,0:T(8,128)(2,1)} %lroot.1, ...), custom_call_target="tpu_custom_call" | custom-call | tf_op jit(solution)/shard_map/shampoo/pallas_call | solution.py:297
  68.1 4.0 %write_out.1 = (bf16[256,4096]{1,0:T(8,128)(2,1)}, f32[1,1024,1024]{2,1,0:T(8,128)}, f32[1,1024,1024]{2,1,0:T(8,128)}) custom-call(bf16[4,256,1024]{2,1,0:T(8,128)(2,1)S(1)} %get-tuple-element.6.upd, f32[1024,1024]{1,0:T(8,128)S(1)} %get-tuple-element.7.nl, f32[1024,1024]{1,0:T(8,128)S(1)} %get-tuple-element.8.nr), custom_call_target="tpu_custom_call" | custom-call | tf_op jit(solution)/shard_map/write_out/pallas_call | solution.py:329

commit v3 on v2

--- a/solution.py
+++ b/solution.py
@@ -11,6 +11,9 @@
 ROWS = B // GROUP
 W = 128
 CHUNKS = B // W
+HALVES = 1
+PART = ROWS // HALVES
+STEPS = CHUNKS * HALVES
 PANEL = 256
 AHEAD = 3
 MESH = pl.DeviceIdType.MESH
@@ -23,7 +26,7 @@
 def kernel(slot_hbm, grad, lf, rf, lroot, rroot, upd, nl, nr, *scratch):
     scratch = list(scratch)
     take = lambda n: [scratch.pop(0) for _ in range(n)]
-    zr, yst, yr, zst = take(CHUNKS), take(CHUNKS), take(CHUNKS), take(CHUNKS)
+    zr, yst, yr, zst = take(STEPS), take(STEPS), take(STEPS), take(STEPS)
     g, gt, half, pst, lv, rv, gsq, psq, sc_out, sc_in = take(10)
     slot, slot_sem, acc = take(3)
     load_sem, own_sem, z_send, z_recv, y_send, y_recv = take(6)
@@ -45,14 +48,27 @@
         )
     ]
 
+    def part_rows(c):
+        return pl.ds(c % HALVES * PART, PART)
+
+    def block_rows(q, c):
+        return pl.ds(pl.multiple_of(q * ROWS + c % HALVES * PART, PART), PART)
+
+    def part_cols(c):
+        return pl.ds(c // HALVES * W, W)
+
     def own_copy(c):
         return pltpu.make_async_copy(
-            grad.at[:, pl.ds(pl.multiple_of(z * B + c * W, W), W)], zr[c].at[z], own_sem.at[c]
+            grad.at[part_rows(c), pl.ds(pl.multiple_of(z * B + c // HALVES * W, W), W)],
+            zr[c].at[z],
+            own_sem.at[c],
         )
 
     def z_copy(c, o):
         return pltpu.make_async_remote_copy(
-            src_ref=grad.at[:, pl.ds(pl.multiple_of(z_peers[o] * B + c * W, W), W)],
+            src_ref=grad.at[
+                part_rows(c), pl.ds(pl.multiple_of(z_peers[o] * B + c // HALVES * W, W), W)
+            ],
             dst_ref=zr[c].at[z],
             send_sem=z_send.at[c, o],
             recv_sem=z_recv.at[c, o],
@@ -63,7 +79,7 @@
     def y_copy(c, o):
         return pltpu.make_async_remote_copy(
             src_ref=yst[c].at[o - 1],
-            dst_ref=g.at[pl.ds(pl.multiple_of(m * ROWS, ROWS), ROWS), pl.ds(c * W, W)],
+            dst_ref=g.at[block_rows(m, c), part_cols(c)],
             send_sem=y_send.at[c, o],
             recv_sem=y_recv.at[c, o],
             device_id=m_dev[o],
@@ -72,7 +88,7 @@
 
     def by_copy(c, o):
         return pltpu.make_async_remote_copy(
-            src_ref=pst.at[pl.ds(pl.multiple_of(m_peers[o] * ROWS, ROWS), ROWS), pl.ds(c * W, W)],
+            src_ref=pst.at[block_rows(m_peers[o], c), part_cols(c)],
             dst_ref=yr[c].at[m],
             send_sem=by_send.at[c, o],
             recv_sem=by_recv.at[c, o],
@@ -93,7 +109,7 @@
     def bz_copy(c, o):
         return pltpu.make_async_remote_copy(
             src_ref=zst[c].at[o - 1],
-            dst_ref=upd.at[z, :, pl.ds(c * W, W)],
+            dst_ref=upd.at[z, part_rows(c), part_cols(c)],
             send_sem=bz_send.at[c, o],
             recv_sem=bz_recv.at[c, o],
             device_id=z_dev[o],
@@ -124,7 +140,6 @@
 
     gsq[...] = jnp.zeros_like(gsq)
     psq[...] = jnp.zeros_like(psq)
-    mine = pl.ds(pl.multiple_of(m * ROWS, ROWS), ROWS)
 
     def relay(c):
         own_copy(c).wait()
@@ -133,11 +148,12 @@
         for o in (1, 2, 3):
             yst[c][o - 1] = zr[c][slot[z, m_peers[o], row_block]]
             y_copy(c, o).start()
-        g[mine, pl.ds(c * W, W)] = zr[c][slot[z, m, row_block]]
+        g[block_rows(m, c), part_cols(c)] = zr[c][slot[z, m, row_block]]
 
     def left_product(c):
-        for o in (1, 2, 3):
-            y_copy(c, o).wait_recv()
+        for h in range(HALVES):
+            for o in (1, 2, 3):
+                y_copy(c * HALVES + h, o).wait_recv()
         cols = pl.ds(c * W, W)
 
         @pl.loop(0, B, step=PANEL, unroll=True)
@@ -159,9 +175,10 @@
             acc[rows, :] = part if start == 0 else acc[rows, :] + part
 
     for c in range(CHUNKS):
-        relay(c)
-        if c + AHEAD < CHUNKS:
-            send_z(c + AHEAD)
+        for k in range(c * HALVES, (c + 1) * HALVES):
+            relay(k)
+            if k + AHEAD < STEPS:
+                send_z(k + AHEAD)
         if c == 1:
             loads[0].wait()
         if c >= 2:
@@ -178,8 +195,8 @@
 
     inner = pl.ds(7 * W, W)
 
-    def right_product(p):
-        cols = pl.ds(p * PANEL, PANEL)
+    def right_product(start, width):
+        cols = pl.ds(start, width)
 
         @pl.loop(0, B, step=PANEL, unroll=True)
         def _(r):
@@ -188,18 +205,21 @@
                 half[rows, inner], rv[inner, cols], preferred_element_type=jnp.float32
             )
             square = part * part
-            psq[...] += fold(square[:, :128]) + fold(square[:, 128:])
+            for j in range(0, width, 128):
+                psq[...] += fold(square[:, j : j + 128])
             pst[rows, cols] = part.astype(jnp.bfloat16)
 
     def send_back(c):
         for o in (1, 2, 3):
             by_copy(c, o).start()
-        yr[c][m] = pst[mine, pl.ds(c * W, W)]
-
-    right_product(0)
-    send_back(0)
+        yr[c][m] = pst[block_rows(m, c), part_cols(c)]
+
+    right_product(0, W)
+    for k in range(HALVES):
+        send_back(k)
+    right_product(W, W)
     for p in range(1, B // PANEL):
-        right_product(p)
+        right_product(p * PANEL, PANEL)
     count = 1.0 / (B * B)
     grad_mean = jnp.sum(gsq[...], axis=(0, 1), keepdims=True) * count
     pre_mean = jnp.sum(psq[...], axis=(0, 1), keepdims=True) * count
@@ -208,8 +228,8 @@
     sc_in[m] = scale
     for o in (1, 2, 3):
         sc_copy(o).start()
-    for c in range(1, CHUNKS):
-        send_back(c)
+    for k in range(HALVES, STEPS):
+        send_back(k)
 
     def left_gram(p):
         cols = pl.ds(p * PANEL, PANEL)
@@ -252,27 +272,27 @@
                 zst[c][o - 1] = piece
                 bz_copy(c, o).start()
             else:
-                upd[z, :, pl.ds(c * W, W)] = piece
+                upd[z, part_rows(c), part_cols(c)] = piece
 
     for o in (1, 2, 3):
         sc_copy(o).wait_recv()
-    for c in range(CHUNKS):
-        relay_back(c)
-        if c < 4:
-            left_gram(c)
+    for k in range(STEPS):
+        relay_back(k)
+        if k < 4:
+            left_gram(k)
         else:
-            right_gram(c - 4)
-        for o in (1, 2, 3):
-            z_copy(c, o).wait_send()
-            y_copy(c, o).wait_send()
-            if c:
-                by_copy(c - 1, o).wait_send()
+            right_gram(k - 4)
+        for o in (1, 2, 3):
+            z_copy(k, o).wait_send()
+            y_copy(k, o).wait_send()
+            if k:
+                by_copy(k - 1, o).wait_send()
     for o in (1, 2, 3):
         sc_copy(o).wait_send()
-        by_copy(CHUNKS - 1, o).wait_send()
-    for c in range(CHUNKS):
-        for o in (1, 2, 3):
-            bz_copy(c, o).wait()
+        by_copy(STEPS - 1, o).wait_send()
+    for k in range(STEPS):
+        for o in (1, 2, 3):
+            bz_copy(k, o).wait()
 
 
 def write_out(upd, nl, nr, update, new_left, new_right, sem):
@@ -303,19 +323,19 @@
         ),
         in_specs=[hbm, hbm, hbm, hbm, hbm, hbm],
         out_specs=(vmem, vmem, vmem),
-        scratch_shapes=[pltpu.VMEM((4, ROWS, W), bf16)] * CHUNKS
-        + [pltpu.VMEM((3, ROWS, W), bf16)] * CHUNKS
-        + [pltpu.VMEM((4, ROWS, W), bf16)] * CHUNKS
-        + [pltpu.VMEM((3, ROWS, W), bf16)] * CHUNKS
+        scratch_shapes=[pltpu.VMEM((4, PART, W), bf16)] * STEPS
+        + [pltpu.VMEM((3, PART, W), bf16)] * STEPS
+        + [pltpu.VMEM((4, PART, W), bf16)] * STEPS
+        + [pltpu.VMEM((3, PART, W), bf16)] * STEPS
         + [pltpu.VMEM((B, B), bf16)] * 6
         + [pltpu.VMEM((8, 128), f32)] * 3
         + [pltpu.VMEM((4, 8, 128), f32)]
         + [pltpu.SMEM((TENSORS, GROUP, block_slot.shape[0]), jnp.int32), dma]
         + [pltpu.VMEM((B, B), f32)]
-        + [dma((4,)), dma((CHUNKS,))]
-        + [dma((CHUNKS, 4))] * 6
+        + [dma((4,)), dma((STEPS,))]
+        + [dma((STEPS, 4))] * 6
         + [dma((4,))] * 2
-        + [dma((CHUNKS, 4))] * 2,
+        + [dma((STEPS, 4))] * 2,
         compiler_params=pltpu.CompilerParams(
             collective_id=0, has_side_effects=True, vmem_limit_bytes=32 * 2**20
         ),

time: 73.3 us -> 73.2 us (level)
  no operation moved by 1% of the time
where the time goes in v3:
time: 73.2 us; the launch traced here: 72.2 us
  Pallas kernels  71.4 us (98%)
  between operations  0.8 us (1%)
    pallas_call x1, Pallas kernels, per_device(): pl.pallas_call(kernel, out_shape=(pltpu.VMEM((TENSORS, ROWS, B), bf16), p...  67.4 us
    pallas_call x1, Pallas kernels, per_device(): pl.pallas_call(write_out, out_shape=(pltpu.HBM((ROWS, TENSORS * B), bf16)...  4.04 us

profile of v3, /device:TPU:3, one launch (start us, length us, event | category | flops | bytes accessed | tf_op | source)
XLA Modules:
  0.0 72.2 jit_solution(5637245414648037045)
XLA Ops:
  0.6 67.4 %shampoo.1 = (bf16[4,256,1024]{2,1,0:T(8,128)(2,1)S(1)}, f32[1024,1024]{1,0:T(8,128)S(1)}, f32[1024,1024]{1,0:T(8,128)S(1)}) custom-call(s32[4,4,8]{2,1,0:T(4,128)} %bitcast.1, bf16[256,4096]{1,0:T(8,128)(2,1)} %grad.1, f32[1,1024,1024]{2,1,0:T(8,128)} %lf.1, f32[1,1024,1024]{2,1,0:T(8,128)} %rf.1, bf16[1,1024,1024]{2,1,0:T(8,128)(2,1)} %lroot.1, ...), custom_call_target="tpu_custom_call" | custom-call | tf_op jit(solution)/shard_map/shampoo/pallas_call | solution.py:317
  68.0 4.0 %write_out.1 = (bf16[256,4096]{1,0:T(8,128)(2,1)}, f32[1,1024,1024]{2,1,0:T(8,128)}, f32[1,1024,1024]{2,1,0:T(8,128)}) custom-call(bf16[4,256,1024]{2,1,0:T(8,128)(2,1)S(1)} %get-tuple-element.6.upd, f32[1024,1024]{1,0:T(8,128)S(1)} %get-tuple-element.7.nl, f32[1024,1024]{1,0:T(8,128)S(1)} %get-tuple-element.8.nr), custom_call_target="tpu_custom_call" | custom-call | tf_op jit(solution)/shard_map/write_out/pallas_call | solution.py:349

commit v4 on v3

--- a/solution.py
+++ b/solution.py
@@ -11,11 +11,11 @@
 ROWS = B // GROUP
 W = 128
 CHUNKS = B // W
-HALVES = 1
+HALVES = 2
 PART = ROWS // HALVES
 STEPS = CHUNKS * HALVES
 PANEL = 256
-AHEAD = 3
+AHEAD = 6
 MESH = pl.DeviceIdType.MESH
 
 
@@ -70,8 +70,8 @@
                 part_rows(c), pl.ds(pl.multiple_of(z_peers[o] * B + c // HALVES * W, W), W)
             ],
             dst_ref=zr[c].at[z],
-            send_sem=z_send.at[c, o],
-            recv_sem=z_recv.at[c, o],
+            send_sem=z_send.at[c, o - 1],
+            recv_sem=z_recv.at[c, o - 1],
             device_id=z_dev[o],
             device_id_type=MESH,
         )
@@ -80,8 +80,8 @@
         return pltpu.make_async_remote_copy(
             src_ref=yst[c].at[o - 1],
             dst_ref=g.at[block_rows(m, c), part_cols(c)],
-            send_sem=y_send.at[c, o],
-            recv_sem=y_recv.at[c, o],
+            send_sem=y_send.at[c, o - 1],
+            recv_sem=y_recv.at[c, o - 1],
             device_id=m_dev[o],
             device_id_type=MESH,
         )
@@ -90,8 +90,8 @@
         return pltpu.make_async_remote_copy(
             src_ref=pst.at[block_rows(m_peers[o], c), part_cols(c)],
             dst_ref=yr[c].at[m],
-            send_sem=by_send.at[c, o],
-            recv_sem=by_recv.at[c, o],
+            send_sem=by_send.at[c, o - 1],
+            recv_sem=by_recv.at[c, o - 1],
             device_id=m_dev[o],
             device_id_type=MESH,
         )
@@ -110,8 +110,8 @@
         return pltpu.make_async_remote_copy(
             src_ref=zst[c].at[o - 1],
             dst_ref=upd.at[z, part_rows(c), part_cols(c)],
-            send_sem=bz_send.at[c, o],
-            recv_sem=bz_recv.at[c, o],
+            send_sem=bz_send.at[c, o - 1],
+            recv_sem=bz_recv.at[c, o - 1],
             device_id=z_dev[o],
             device_id_type=MESH,
         )
@@ -278,10 +278,10 @@
         sc_copy(o).wait_recv()
     for k in range(STEPS):
         relay_back(k)
-        if k < 4:
-            left_gram(k)
-        else:
-            right_gram(k - 4)
+        if k % 2 == 0 and k < 8:
+            left_gram(k // 2)
+        elif k % 2 == 0 and k < 16:
+            right_gram(k // 2 - 4)
         for o in (1, 2, 3):
             z_copy(k, o).wait_send()
             y_copy(k, o).wait_send()
@@ -333,9 +333,9 @@
         + [pltpu.SMEM((TENSORS, GROUP, block_slot.shape[0]), jnp.int32), dma]
         + [pltpu.VMEM((B, B), f32)]
         + [dma((4,)), dma((STEPS,))]
-        + [dma((STEPS, 4))] * 6
+        + [dma((STEPS, 3))] * 6
         + [dma((4,))] * 2
-        + [dma((STEPS, 4))] * 2,
+        + [dma((STEPS, 3))] * 2,
         compiler_params=pltpu.CompilerParams(
             collective_id=0, has_side_effects=True, vmem_limit_bytes=32 * 2**20
         ),

time: 73.2 us -> 73.7 us (level)
  no operation moved by 1% of the time
where the time goes in v4:
time: 73.7 us; the launch traced here: 72.8 us
  Pallas kernels  72 us (98%)
  between operations  0.8 us (1%)
    pallas_call x1, Pallas kernels, per_device(): pl.pallas_call(kernel, out_shape=(pltpu.VMEM((TENSORS, ROWS, B), bf16), p...  67.9 us
    pallas_call x1, Pallas kernels, per_device(): pl.pallas_call(write_out, out_shape=(pltpu.HBM((ROWS, TENSORS * B), bf16)...  4.04 us

profile of v4, /device:TPU:3, one launch (start us, length us, event | category | flops | bytes accessed | tf_op | source)
XLA Modules:
  0.0 72.8 jit_solution(722681195680933589)
XLA Ops:
  0.6 67.9 %shampoo.1 = (bf16[4,256,1024]{2,1,0:T(8,128)(2,1)S(1)}, f32[1024,1024]{1,0:T(8,128)S(1)}, f32[1024,1024]{1,0:T(8,128)S(1)}) custom-call(s32[4,4,8]{2,1,0:T(4,128)} %bitcast.1, bf16[256,4096]{1,0:T(8,128)(2,1)} %grad.1, f32[1,1024,1024]{2,1,0:T(8,128)} %lf.1, f32[1,1024,1024]{2,1,0:T(8,128)} %rf.1, bf16[1,1024,1024]{2,1,0:T(8,128)(2,1)} %lroot.1, ...), custom_call_target="tpu_custom_call" | custom-call | tf_op jit(solution)/shard_map/shampoo/pallas_call | solution.py:317
  68.6 4.0 %write_out.1 = (bf16[256,4096]{1,0:T(8,128)(2,1)}, f32[1,1024,1024]{2,1,0:T(8,128)}, f32[1,1024,1024]{2,1,0:T(8,128)}) custom-call(bf16[4,256,1024]{2,1,0:T(8,128)(2,1)S(1)} %get-tuple-element.6.upd, f32[1024,1024]{1,0:T(8,128)S(1)} %get-tuple-element.7.nl, f32[1024,1024]{1,0:T(8,128)S(1)} %get-tuple-element.8.nr), custom_call_target="tpu_custom_call" | custom-call | tf_op jit(solution)/shard_map/write_out/pallas_call | solution.py:349
